TPU v7x, 256 devices: a whole 4x4x8 slice. The times are simulated.
256 devices in a mesh: seq: 32 (over y, x, core), head: 8 (over z).
Axes of the slice: x: 4, y: 4, z: 8, core: 2. Of those that a mesh axis runs over, the one named last changes fastest.
Arguments:
- queries: bfloat16 [32, 128, 16384], P('seq', None, 'head'), parts along dimension 2
- cache_keys: bfloat16 [262144, 1024], P('seq', 'head'), parts along dimension 1
- cache_values: bfloat16 [262144, 1024], P('seq', 'head'), parts along dimension 1
- lengths: int32 [32], replicated, may hold values from 1 to 8192, as said below
- span_owner: int32 [1], replicated, may hold values from 0 to 31
Outputs:
- attended: bfloat16 [32, 128, 16384], P('seq', None, 'head'), parts along dimension 2
There are 8 independent parts, one for each index of `head`. A program takes and returns all parts, laid end to end along the dimension named above; an argument that names none is the same for every part. Nothing has to cross between parts.
Inputs may be any that keep to these rules, and one draw needn't show every extreme that they name: `lengths`: every shard but the last holds 8192 valid positions.
All inputs are finite; a program needn't handle non-finite values.
Results may differ from a plain program's by a relative error of at most 0.0019.
Values may be sent and summed in bfloat16 or wider, within the bound.
No kernel may reach another device: no remote copies, remote signals or barrier semaphores. Data moves between devices by JAX's collectives and lax.ppermute only.
A program may use at most 128 MiB of HBM per device.

v0:
```python
import jax
import jax.numpy as jnp
from jax import lax
from jax.sharding import PartitionSpec as P


def spread(array, axis, root):
    mine = lax.axis_index(axis) == root
    return lax.psum(jnp.where(mine, array, jnp.zeros_like(array)), axis)


def combined_all(part, axis, combine):
    gathered = jax.tree.map(lambda a: lax.all_gather(a, axis), part)

    def take(source):
        return jax.tree.map(lambda a: lax.dynamic_index_in_dim(a, source, 0, False), gathered)

    return lax.fori_loop(
        1, lax.axis_size(axis), lambda source, state: combine(state, take(source)), take(0)
    )


def block_partial(query_block, cache_keys, cache_values, valid_len, score_scale):
    scores = (
        lax.dot_general(
            query_block, cache_keys, (((1,), (1,)), ((), ())), preferred_element_type=jnp.float32
        )
        * score_scale
    )
    columns = jnp.arange(cache_keys.shape[0], dtype=jnp.int32)
    scores = jnp.where(columns[None, :] < valid_len, scores, -jnp.inf)
    row_max = jnp.max(scores, axis=1)
    weights = jnp.exp(scores - row_max[:, None])
    row_sum = jnp.sum(weights, axis=1)
    weighted = jnp.dot(
        weights.astype(jnp.bfloat16), cache_values, preferred_element_type=jnp.float32
    )
    return (row_max, row_sum, weighted)


def combine(first, second):
    top = jnp.maximum(first[0], second[0])
    left = jnp.exp(first[0] - top)
    right = jnp.exp(second[0] - top)
    return (
        top,
        left * first[1] + right * second[1],
        left[:, None] * first[2] + right[:, None] * second[2],
    )


def per_device(queries, cache_keys, cache_values, lengths, span_owner):
    device_index = lax.axis_index("seq")
    owner_index = span_owner[0]
    valid_len = lengths[device_index]
    head_size = cache_keys.shape[1]
    block = spread(queries, "seq", owner_index)
    span_len = queries.shape[1]
    total_rows = span_len * queries.shape[2] // head_size
    block_rows = min(512, total_rows)
    query_blocks = block.reshape(total_rows // block_rows, block_rows, head_size)
    score_scale = 1.0 / jnp.sqrt(jnp.float32(head_size))

    def one_block(query_block):
        return block_partial(query_block, cache_keys, cache_values, valid_len, score_scale)

    row_max, row_sum, weighted = lax.map(one_block, query_blocks)
    row_max = row_max.reshape(total_rows)
    row_sum = row_sum.reshape(total_rows)
    weighted = weighted.reshape(total_rows, head_size)
    top, denom, numer = combined_all((row_max, row_sum, weighted), "seq", combine)
    result = (numer / denom[:, None]).astype(jnp.bfloat16).reshape(1, span_len, queries.shape[2])
    return jnp.where(device_index == owner_index, result, jnp.zeros_like(result))


def solution(mesh):
    return jax.shard_map(
        per_device,
        mesh=mesh,
        in_specs=(P("seq", None, "head"), P("seq", "head"), P("seq", "head"), P(), P()),
        out_specs=P("seq", None, "head"),
        check_vma=False,
    )
```

profile of v0, /device:TPU:1, one launch (start us, length us, event | category | flops | bytes accessed | tf_op | source)
XLA Modules:
  0.0 445.9 jit_solution(10816783090056473754)
XLA Ops:
  9.7 118.2 %all-reduce.2.cloned.1.call-done = bf16[4,512,128]{2,1,0:T(8,128)(2,1)} async-done(((bf16[4,512,128]{2,1,0:T(8,128)(2,1)}), bf16[4,512,128]{2,1,0:T(8,128)(2,1)}) %all-reduce.2.cloned.1.call-update) | async-done | bytes 524304 | tf_op jit(solution)/shard_map/psum | solution.py:9
  127.9 122.1 %while.33 = (s32[]{:T(128)}, f32[4,512]{1,0:T(4,128)S(1)}, f32[4,512]{1,0:T(4,128)S(1)}, f32[4,512,128]{2,1,0:T(8,128)}, s32[]{:T(128)}, /*index=5*/bf16[4,512,1...) while((s32[]{:T(128)}, f32[4,512]{1,0:T(4,128)S(1)}, ...), condition=%wide.region_4.5_spmd, body=%wide.region_1.4_spmd.sunk | while | flops 2193628160 | bytes 63357084 | solution.py:67
  128.6 10.2 %fusion.32 = (f32[512]{0:T(512)S(1)}, f32[512,8192]{1,0:T(8,128)}) fusion(pred[8192]{0:T(1024)(128)(4,1)S(1)} %iota_compare_fusion.2, bf16[8192,128]{1,0:T(8,128)(2,1)} %get-tuple-element.403, bf16[4,512,128]{2,1,0:T(8,128)(2,1)} %get-tuple-element.402, s32[]{:T(128)S(6)} %copy.20), kind=kOutput, calls=%fused_computation.2.clone.1 | convolution fusion | flops 1086324224 | bytes 19015684 | tf_op jit(solution)/shard_map/while/body/eval_jaxpr/dot_general | solution.py:25
  138.8 9.8 %fusion.33 = f32[512]{0:T(512)S(1)} fusion(f32[512,8192]{1,0:T(8,128)} %get-tuple-element.363, f32[512]{0:T(512)S(1)} %get-tuple-element.362, pred[8192]{0:T(1024)(128)(4,1)S(1)} %iota_compare_fusion.2), kind=kLoop, calls=%fused_computation.4.clone.1 | loop fusion | flops 16776704 | bytes 16789504 | tf_op jit(solution)/shard_map/while/body/eval_jaxpr/reduce_sum | solution.py:34
  148.6 9.7 %fusion.34 = f32[4,512,128]{2,1,0:T(8,128)} fusion(f32[4,512,128]{2,1,0:T(8,128)} %get-tuple-element.390, s32[]{:T(128)S(6)} %copy.20, bf16[8192,128]{1,0:T(8,128)(2,1)S(1)} %copy-done, f32[512,8192]{1,0:T(8,128)} %get-tuple-element.363, f32[512]{0:T(512)S(1)} %get-tuple-element.362, pred[8192]{0:T(1024)(128)(4,1)S(1)} %iota_compare_fusion.2), kind=kOutput, calls=%fused_computation.8.clone.1 | convolution fusion | flops 1090519040 | bytes 19146756 | tf_op jit(solution)/shard_map/while/body/eval_jaxpr/dot_general | solution.py:35
  159.2 10.2 %fusion.32 = (f32[512]{0:T(512)S(1)}, f32[512,8192]{1,0:T(8,128)}) fusion(pred[8192]{0:T(1024)(128)(4,1)S(1)} %iota_compare_fusion.2, bf16[8192,128]{1,0:T(8,128)(2,1)} %get-tuple-element.403, bf16[4,512,128]{2,1,0:T(8,128)(2,1)} %get-tuple-element.402, s32[]{:T(128)S(6)} %copy.20), kind=kOutput, calls=%fused_computation.2.clone.1 | convolution fusion | flops 1086324224 | bytes 19015684 | tf_op jit(solution)/shard_map/while/body/eval_jaxpr/dot_general | solution.py:25
  169.4 9.8 %fusion.33 = f32[512]{0:T(512)S(1)} fusion(f32[512,8192]{1,0:T(8,128)} %get-tuple-element.363, f32[512]{0:T(512)S(1)} %get-tuple-element.362, pred[8192]{0:T(1024)(128)(4,1)S(1)} %iota_compare_fusion.2), kind=kLoop, calls=%fused_computation.4.clone.1 | loop fusion | flops 16776704 | bytes 16789504 | tf_op jit(solution)/shard_map/while/body/eval_jaxpr/reduce_sum | solution.py:34
  179.2 9.7 %fusion.34 = f32[4,512,128]{2,1,0:T(8,128)} fusion(f32[4,512,128]{2,1,0:T(8,128)} %get-tuple-element.390, s32[]{:T(128)S(6)} %copy.20, bf16[8192,128]{1,0:T(8,128)(2,1)S(1)} %copy-done, f32[512,8192]{1,0:T(8,128)} %get-tuple-element.363, f32[512]{0:T(512)S(1)} %get-tuple-element.362, pred[8192]{0:T(1024)(128)(4,1)S(1)} %iota_compare_fusion.2), kind=kOutput, calls=%fused_computation.8.clone.1 | convolution fusion | flops 1090519040 | bytes 19146756 | tf_op jit(solution)/shard_map/while/body/eval_jaxpr/dot_general | solution.py:35
  189.7 10.2 %fusion.32 = (f32[512]{0:T(512)S(1)}, f32[512,8192]{1,0:T(8,128)}) fusion(pred[8192]{0:T(1024)(128)(4,1)S(1)} %iota_compare_fusion.2, bf16[8192,128]{1,0:T(8,128)(2,1)} %get-tuple-element.403, bf16[4,512,128]{2,1,0:T(8,128)(2,1)} %get-tuple-element.402, s32[]{:T(128)S(6)} %copy.20), kind=kOutput, calls=%fused_computation.2.clone.1 | convolution fusion | flops 1086324224 | bytes 19015684 | tf_op jit(solution)/shard_map/while/body/eval_jaxpr/dot_general | solution.py:25
  199.9 9.8 %fusion.33 = f32[512]{0:T(512)S(1)} fusion(f32[512,8192]{1,0:T(8,128)} %get-tuple-element.363, f32[512]{0:T(512)S(1)} %get-tuple-element.362, pred[8192]{0:T(1024)(128)(4,1)S(1)} %iota_compare_fusion.2), kind=kLoop, calls=%fused_computation.4.clone.1 | loop fusion | flops 16776704 | bytes 16789504 | tf_op jit(solution)/shard_map/while/body/eval_jaxpr/reduce_sum | solution.py:34
  209.7 9.7 %fusion.34 = f32[4,512,128]{2,1,0:T(8,128)} fusion(f32[4,512,128]{2,1,0:T(8,128)} %get-tuple-element.390, s32[]{:T(128)S(6)} %copy.20, bf16[8192,128]{1,0:T(8,128)(2,1)S(1)} %copy-done, f32[512,8192]{1,0:T(8,128)} %get-tuple-element.363, f32[512]{0:T(512)S(1)} %get-tuple-element.362, pred[8192]{0:T(1024)(128)(4,1)S(1)} %iota_compare_fusion.2), kind=kOutput, calls=%fused_computation.8.clone.1 | convolution fusion | flops 1090519040 | bytes 19146756 | tf_op jit(solution)/shard_map/while/body/eval_jaxpr/dot_general | solution.py:35
  220.2 10.2 %fusion.32 = (f32[512]{0:T(512)S(1)}, f32[512,8192]{1,0:T(8,128)}) fusion(pred[8192]{0:T(1024)(128)(4,1)S(1)} %iota_compare_fusion.2, bf16[8192,128]{1,0:T(8,128)(2,1)} %get-tuple-element.403, bf16[4,512,128]{2,1,0:T(8,128)(2,1)} %get-tuple-element.402, s32[]{:T(128)S(6)} %copy.20), kind=kOutput, calls=%fused_computation.2.clone.1 | convolution fusion | flops 1086324224 | bytes 19015684 | tf_op jit(solution)/shard_map/while/body/eval_jaxpr/dot_general | solution.py:25
  230.4 9.8 %fusion.33 = f32[512]{0:T(512)S(1)} fusion(f32[512,8192]{1,0:T(8,128)} %get-tuple-element.363, f32[512]{0:T(512)S(1)} %get-tuple-element.362, pred[8192]{0:T(1024)(128)(4,1)S(1)} %iota_compare_fusion.2), kind=kLoop, calls=%fused_computation.4.clone.1 | loop fusion | flops 16776704 | bytes 16789504 | tf_op jit(solution)/shard_map/while/body/eval_jaxpr/reduce_sum | solution.py:34
  240.2 9.7 %fusion.34 = f32[4,512,128]{2,1,0:T(8,128)} fusion(f32[4,512,128]{2,1,0:T(8,128)} %get-tuple-element.390, s32[]{:T(128)S(6)} %copy.20, bf16[8192,128]{1,0:T(8,128)(2,1)S(1)} %copy-done, f32[512,8192]{1,0:T(8,128)} %get-tuple-element.363, f32[512]{0:T(512)S(1)} %get-tuple-element.362, pred[8192]{0:T(1024)(128)(4,1)S(1)} %iota_compare_fusion.2), kind=kOutput, calls=%fused_computation.8.clone.1 | convolution fusion | flops 1090519040 | bytes 19146756 | tf_op jit(solution)/shard_map/while/body/eval_jaxpr/dot_general | solution.py:35
  250.1 26.0 %all-gather.1 = f32[32,1,2048]{2,1,0:T(1,128)S(1)} all-gather(f32[1,1,2048]{2,1,0:T(1,128)S(1)} %reshape.31), channel_id=1, replica_groups=mesh['seq'=32,'head'=8] {'seq'}, dimensions={0}, use_global_device_ids=true | all-gather | bytes 270336 | tf_op jit(solution)/shard_map/all_gather | solution.py:13
  276.2 22.1 %all-gather = f32[32,1,2048]{2,1,0:T(1,128)S(1)} all-gather(f32[1,1,2048]{2,1,0:T(1,128)S(1)} %reshape.29), channel_id=1, replica_groups=mesh['seq'=32,'head'=8] {'seq'}, dimensions={0}, use_global_device_ids=true | all-gather | bytes 270336 | tf_op jit(solution)/shard_map/all_gather | solution.py:13
  298.4 71.1 %all-gather.4.cloned.1.call-done = f32[32,2048,128]{2,1,0:T(8,128)} async-done(((f32[1,2048,128]{2,1,0:T(8,128)}), f32[32,2048,128]{2,1,0:T(8,128)}) %all-gather.4.cloned.1.call-update) | async-done | bytes 33554448 | tf_op jit(solution)/shard_map/all_gather | solution.py:13
  370.7 67.0 %while.34 = (s32[]{:T(128)}, f32[2048]{0:T(1024)S(1)}, f32[2048]{0:T(1024)S(1)}, f32[2048,128]{1,0:T(8,128)S(1)}, f32[32,2048]{1,0:T(8,128)S(1)}, /*index=5*/f32...) while((s32[]{:T(128)}, f32[2048]{0:T(1024)S(1)}, f32[2048]{0:T(1024)S(1)}, ...), condition=%wide.region_6.7_spmd, body=%wide.region_5.6_spmd.sunk | while | flops 798725 | bytes 3260559 | solution.py:18
  370.8 2.1 fusion.35
  373.0 2.1 fusion.35
  375.1 2.1 fusion.35
  377.3 2.1 fusion.35
  379.5 2.1 fusion.35
  381.6 2.1 fusion.35
  (126 shorter events, 61.7 us)
Async XLA Ops:
  6.5 121.4 %all-reduce.2.cloned.1.call-start = ((), (), s32[]{:S(2)}) async-start(), calls=%async_computation | async-start | bytes 1048576 | tf_op jit(solution)/shard_map/psum | solution.py:9
  8.3 361.1 %all-gather.4.cloned.1.call-start = ((), (), s32[]{:S(2)}) async-start(), calls=%async_computation.1 | async-start | bytes 34603008 | tf_op jit(solution)/shard_map/all_gather | solution.py:13
  128.6 20.0 %copy-start = (bf16[8192,128]{1,0:T(8,128)(2,1)S(1)}, bf16[8192,128]{1,0:T(8,128)(2,1)}, u32[]{:S(2)}) copy-start(bf16[8192,128]{1,0:T(8,128)(2,1)} %get-tuple-element.404) | copy-start | bytes 6291460 | tf_op jit(solution)/shard_map/while
  159.2 20.0 %copy-start = (bf16[8192,128]{1,0:T(8,128)(2,1)S(1)}, bf16[8192,128]{1,0:T(8,128)(2,1)}, u32[]{:S(2)}) copy-start(bf16[8192,128]{1,0:T(8,128)(2,1)} %get-tuple-element.404) | copy-start | bytes 6291460 | tf_op jit(solution)/shard_map/while
  189.7 20.0 %copy-start = (bf16[8192,128]{1,0:T(8,128)(2,1)S(1)}, bf16[8192,128]{1,0:T(8,128)(2,1)}, u32[]{:S(2)}) copy-start(bf16[8192,128]{1,0:T(8,128)(2,1)} %get-tuple-element.404) | copy-start | bytes 6291460 | tf_op jit(solution)/shard_map/while
  220.2 20.0 %copy-start = (bf16[8192,128]{1,0:T(8,128)(2,1)S(1)}, bf16[8192,128]{1,0:T(8,128)(2,1)}, u32[]{:S(2)}) copy-start(bf16[8192,128]{1,0:T(8,128)(2,1)} %get-tuple-element.404) | copy-start | bytes 6291460 | tf_op jit(solution)/shard_map/while
Sparse Core Ops, SparseCore 0:
  10.5 117.3 all-reduce.1
  250.2 119.2 all-gather.3
where the time goes:
time: 448 us; the launch traced here: 446 us
  waiting for transfers between devices  189 us (42%)
  other arithmetic  107 us (24%)
  matrix products  79.7 us (18%)
  blocking collectives  48.1 us (11%)
  between operations  14.1 us (3%)
  local copies, waits for them, and re-layouts  5.85 us (1%)
    psum x1, waiting for transfers between devices, spread(): return lax.psum(jnp.where(mine, array, jnp.zeros_like(array)), axis)  118 us
    all_gather x1, waiting for transfers between devices, combined_all(): gathered = jax.tree.map(lambda a: lax.all_gather(a, axis), part)  71.1 us
    add x31, other arithmetic, combine(): left[:, None] * first[2] + right[:, None] * second[2]  64.7 us
    all_gather x2, blocking collectives, combined_all(): gathered = jax.tree.map(lambda a: lax.all_gather(a, axis), part)  48.1 us
    dot_general x4, matrix products, block_partial(): lax.dot_general(query_block, cache_keys, (((1,), (1,)), ((), ())), prefer...  40.8 us
    reduce_sum x4, other arithmetic, block_partial(): row_sum = jnp.sum(weights, axis=1)  39.2 us
    dot_general x4, matrix products, block_partial(): jnp.dot(weights.astype(jnp.bfloat16), cache_values, preferred_element_typ...  38.9 us
  transfers between devices with their start and end apart: 2, of which 2 were waited for; matrix products, arithmetic and copies ran while one was open for 0% of the time, Pallas kernels for 0%

commit v1 on v0

--- a/solution.py
+++ b/solution.py
@@ -6,7 +6,7 @@
 
 def spread(array, axis, root):
     mine = lax.axis_index(axis) == root
-    return lax.psum(jnp.where(mine, array, jnp.zeros_like(array)), axis)
+    return jnp.sum(lax.all_gather(jnp.where(mine, array, jnp.zeros_like(array)), axis), axis=0)
 
 
 def combined_all(part, axis, combine):

time: 448 us -> 410 us (0.915)
  waiting for transfers between devices: 189 us -> 154 us
  matrix products: 79.7 us -> 69.5 us
  other arithmetic: 107 us -> 117 us
    psum x1 -> x0, waiting for transfers between devices: 118 us -> none  [spread(): return lax.psum(jnp.where(mine, array, jnp.zeros_like(array)), axis)]
    all_gather x0 -> x1, waiting for transfers between devices: none -> 82.1 us  [spread(): lax.all_gather(jnp.where(mine, array, jnp.zeros_like(array)), axis)]
    dot_general x4, matrix products: 40.8 us -> 28.2 us  [block_partial(): lax.dot_general(query_block, cache_keys, (((1,), (1,)), ((), ())), prefer...]
    reduce_sum x0 -> x1, other arithmetic: none -> 8.86 us  [spread(): jnp.sum(lax.all_gather(jnp.where(mine, array, jnp.zeros_like(array)), axi...]
where the time goes in v1:
time: 410 us; the launch traced here: 408 us
  waiting for transfers between devices  154 us (38%)
  other arithmetic  117 us (29%)
  matrix products  69.5 us (17%)
  blocking collectives  47.3 us (12%)
  between operations  14.3 us (3%)
  local copies, waits for them, and re-layouts  4.98 us (1%)
    all_gather x1, waiting for transfers between devices, spread(): lax.all_gather(jnp.where(mine, array, jnp.zeros_like(array)), axis)  82.1 us
    all_gather x1, waiting for transfers between devices, combined_all(): gathered = jax.tree.map(lambda a: lax.all_gather(a, axis), part)  71.4 us
    add x31, other arithmetic, combine(): left[:, None] * first[2] + right[:, None] * second[2]  64.7 us
    all_gather x2, blocking collectives, combined_all(): gathered = jax.tree.map(lambda a: lax.all_gather(a, axis), part)  47.3 us
    dot_general x4, matrix products, block_partial(): jnp.dot(weights.astype(jnp.bfloat16), cache_values, preferred_element_typ...  41.3 us
    reduce_sum x4, other arithmetic, block_partial(): row_sum = jnp.sum(weights, axis=1)  39.2 us
    dot_general x4, matrix products, block_partial(): lax.dot_general(query_block, cache_keys, (((1,), (1,)), ((), ())), prefer...  28.2 us
    reduce_sum x1, other arithmetic, spread(): jnp.sum(lax.all_gather(jnp.where(mine, array, jnp.zeros_like(array)), axi...  8.86 us
  transfers between devices with their start and end apart: 2, of which 2 were waited for; matrix products, arithmetic and copies ran while one was open for 0% of the time, Pallas kernels for 0%

profile of v1, /device:TPU:1, one launch (start us, length us, event | category | flops | bytes accessed | tf_op | source)
XLA Modules:
  0.0 407.9 jit_solution(12268753457291387873)
XLA Ops:
  9.5 82.1 %all-gather.8.cloned.1.call-done = bf16[32,128,2048]{2,1,0:T(8,128)(2,1)} async-done(((bf16[1,128,2048]{2,1,0:T(8,128)(2,1)}), bf16[32,128,2048]{2,1,0:T(8,128)(2,1)}) %all-gather.8.cloned.1.call-update) | async-done | bytes 16777232 | tf_op jit(solution)/shard_map/all_gather | solution.py:9
  91.7 8.9 %reduce.2 = bf16[128,2048]{1,0:T(8,128)(2,1)S(1)} reduce(bf16[32,128,2048]{2,1,0:T(8,128)(2,1)} %all-gather.8.cloned.1.call-done, bf16[]{:T(256)} %constant.84.clone.1), dimensions={0}, to_apply=%region_0.1 | reduce | flops 8126464 | bytes 17301506 | tf_op jit(solution)/shard_map/reduce_sum | solution.py:9
  100.8 111.7 %while.33 = (s32[]{:T(128)}, f32[4,512]{1,0:T(4,128)S(1)}, f32[4,512]{1,0:T(4,128)S(1)}, f32[4,512,128]{2,1,0:T(8,128)}, s32[]{:T(128)}, /*index=5*/bf16[4,512,1...) while((s32[]{:T(128)}, f32[4,512]{1,0:T(4,128)S(1)}, ...), condition=%wide.region_4.5_spmd, body=%wide.region_1.4_spmd.sunk | while | flops 2193628160 | bytes 54968448 | solution.py:67
  101.4 7.1 %fusion.32 = (f32[512]{0:T(512)S(1)}, f32[512,8192]{1,0:T(8,128)}) fusion(pred[8192]{0:T(1024)(128)(4,1)S(1)} %iota_compare_fusion.2, bf16[8192,128]{1,0:T(8,128)(2,1)S(1)} %get-tuple-element.403, bf16[4,512,128]{2,1,0:T(8,128)(2,1)S(1)} %get-tuple-element.402, s32[]{:T(128)S(6)} %copy.19), kind=kOutput, calls=%fused_computation.2.clone.1 | convolution fusion | flops 1086324224 | bytes 19015684 | tf_op jit(solution)/shard_map/while/body/eval_jaxpr/dot_general | solution.py:25
  108.5 9.8 %fusion.33 = f32[512]{0:T(512)S(1)} fusion(f32[512,8192]{1,0:T(8,128)} %get-tuple-element.363, f32[512]{0:T(512)S(1)} %get-tuple-element.362, pred[8192]{0:T(1024)(128)(4,1)S(1)} %iota_compare_fusion.2), kind=kLoop, calls=%fused_computation.4.clone.1 | loop fusion | flops 16776704 | bytes 16789504 | tf_op jit(solution)/shard_map/while/body/eval_jaxpr/reduce_sum | solution.py:34
  118.3 10.3 %fusion.34 = f32[4,512,128]{2,1,0:T(8,128)} fusion(f32[4,512,128]{2,1,0:T(8,128)} %get-tuple-element.390, s32[]{:T(128)S(6)} %copy.19, bf16[8192,128]{1,0:T(8,128)(2,1)} %get-tuple-element.404, f32[512,8192]{1,0:T(8,128)} %get-tuple-element.363, f32[512]{0:T(512)S(1)} %get-tuple-element.362, pred[8192]{0:T(1024)(128)(4,1)S(1)} %iota_compare_fusion.2), kind=kOutput, calls=%fused_computation.8.clone.1 | convolution fusion | flops 1090519040 | bytes 19146756 | tf_op jit(solution)/shard_map/while/body/eval_jaxpr/dot_general | solution.py:35
  129.4 7.1 %fusion.32 = (f32[512]{0:T(512)S(1)}, f32[512,8192]{1,0:T(8,128)}) fusion(pred[8192]{0:T(1024)(128)(4,1)S(1)} %iota_compare_fusion.2, bf16[8192,128]{1,0:T(8,128)(2,1)S(1)} %get-tuple-element.403, bf16[4,512,128]{2,1,0:T(8,128)(2,1)S(1)} %get-tuple-element.402, s32[]{:T(128)S(6)} %copy.19), kind=kOutput, calls=%fused_computation.2.clone.1 | convolution fusion | flops 1086324224 | bytes 19015684 | tf_op jit(solution)/shard_map/while/body/eval_jaxpr/dot_general | solution.py:25
  136.4 9.8 %fusion.33 = f32[512]{0:T(512)S(1)} fusion(f32[512,8192]{1,0:T(8,128)} %get-tuple-element.363, f32[512]{0:T(512)S(1)} %get-tuple-element.362, pred[8192]{0:T(1024)(128)(4,1)S(1)} %iota_compare_fusion.2), kind=kLoop, calls=%fused_computation.4.clone.1 | loop fusion | flops 16776704 | bytes 16789504 | tf_op jit(solution)/shard_map/while/body/eval_jaxpr/reduce_sum | solution.py:34
  146.2 10.3 %fusion.34 = f32[4,512,128]{2,1,0:T(8,128)} fusion(f32[4,512,128]{2,1,0:T(8,128)} %get-tuple-element.390, s32[]{:T(128)S(6)} %copy.19, bf16[8192,128]{1,0:T(8,128)(2,1)} %get-tuple-element.404, f32[512,8192]{1,0:T(8,128)} %get-tuple-element.363, f32[512]{0:T(512)S(1)} %get-tuple-element.362, pred[8192]{0:T(1024)(128)(4,1)S(1)} %iota_compare_fusion.2), kind=kOutput, calls=%fused_computation.8.clone.1 | convolution fusion | flops 1090519040 | bytes 19146756 | tf_op jit(solution)/shard_map/while/body/eval_jaxpr/dot_general | solution.py:35
  157.3 7.1 %fusion.32 = (f32[512]{0:T(512)S(1)}, f32[512,8192]{1,0:T(8,128)}) fusion(pred[8192]{0:T(1024)(128)(4,1)S(1)} %iota_compare_fusion.2, bf16[8192,128]{1,0:T(8,128)(2,1)S(1)} %get-tuple-element.403, bf16[4,512,128]{2,1,0:T(8,128)(2,1)S(1)} %get-tuple-element.402, s32[]{:T(128)S(6)} %copy.19), kind=kOutput, calls=%fused_computation.2.clone.1 | convolution fusion | flops 1086324224 | bytes 19015684 | tf_op jit(solution)/shard_map/while/body/eval_jaxpr/dot_general | solution.py:25
  164.3 9.8 %fusion.33 = f32[512]{0:T(512)S(1)} fusion(f32[512,8192]{1,0:T(8,128)} %get-tuple-element.363, f32[512]{0:T(512)S(1)} %get-tuple-element.362, pred[8192]{0:T(1024)(128)(4,1)S(1)} %iota_compare_fusion.2), kind=kLoop, calls=%fused_computation.4.clone.1 | loop fusion | flops 16776704 | bytes 16789504 | tf_op jit(solution)/shard_map/while/body/eval_jaxpr/reduce_sum | solution.py:34
  174.1 10.3 %fusion.34 = f32[4,512,128]{2,1,0:T(8,128)} fusion(f32[4,512,128]{2,1,0:T(8,128)} %get-tuple-element.390, s32[]{:T(128)S(6)} %copy.19, bf16[8192,128]{1,0:T(8,128)(2,1)} %get-tuple-element.404, f32[512,8192]{1,0:T(8,128)} %get-tuple-element.363, f32[512]{0:T(512)S(1)} %get-tuple-element.362, pred[8192]{0:T(1024)(128)(4,1)S(1)} %iota_compare_fusion.2), kind=kOutput, calls=%fused_computation.8.clone.1 | convolution fusion | flops 1090519040 | bytes 19146756 | tf_op jit(solution)/shard_map/while/body/eval_jaxpr/dot_general | solution.py:35
  185.2 7.1 %fusion.32 = (f32[512]{0:T(512)S(1)}, f32[512,8192]{1,0:T(8,128)}) fusion(pred[8192]{0:T(1024)(128)(4,1)S(1)} %iota_compare_fusion.2, bf16[8192,128]{1,0:T(8,128)(2,1)S(1)} %get-tuple-element.403, bf16[4,512,128]{2,1,0:T(8,128)(2,1)S(1)} %get-tuple-element.402, s32[]{:T(128)S(6)} %copy.19), kind=kOutput, calls=%fused_computation.2.clone.1 | convolution fusion | flops 1086324224 | bytes 19015684 | tf_op jit(solution)/shard_map/while/body/eval_jaxpr/dot_general | solution.py:25
  192.3 9.8 %fusion.33 = f32[512]{0:T(512)S(1)} fusion(f32[512,8192]{1,0:T(8,128)} %get-tuple-element.363, f32[512]{0:T(512)S(1)} %get-tuple-element.362, pred[8192]{0:T(1024)(128)(4,1)S(1)} %iota_compare_fusion.2), kind=kLoop, calls=%fused_computation.4.clone.1 | loop fusion | flops 16776704 | bytes 16789504 | tf_op jit(solution)/shard_map/while/body/eval_jaxpr/reduce_sum | solution.py:34
  202.0 10.3 %fusion.34 = f32[4,512,128]{2,1,0:T(8,128)} fusion(f32[4,512,128]{2,1,0:T(8,128)} %get-tuple-element.390, s32[]{:T(128)S(6)} %copy.19, bf16[8192,128]{1,0:T(8,128)(2,1)} %get-tuple-element.404, f32[512,8192]{1,0:T(8,128)} %get-tuple-element.363, f32[512]{0:T(512)S(1)} %get-tuple-element.362, pred[8192]{0:T(1024)(128)(4,1)S(1)} %iota_compare_fusion.2), kind=kOutput, calls=%fused_computation.8.clone.1 | convolution fusion | flops 1090519040 | bytes 19146756 | tf_op jit(solution)/shard_map/while/body/eval_jaxpr/dot_general | solution.py:35
  212.5 24.5 %all-gather.2 = f32[32,1,2048]{2,1,0:T(1,128)S(1)} all-gather(f32[1,1,2048]{2,1,0:T(1,128)S(1)} %reshape.35), channel_id=1, replica_groups=mesh['seq'=32,'head'=8] {'seq'}, dimensions={0}, use_global_device_ids=true | all-gather | bytes 270336 | tf_op jit(solution)/shard_map/all_gather | solution.py:13
  237.1 22.8 %all-gather.1 = f32[32,1,2048]{2,1,0:T(1,128)S(1)} all-gather(f32[1,1,2048]{2,1,0:T(1,128)S(1)} %reshape.33), channel_id=1, replica_groups=mesh['seq'=32,'head'=8] {'seq'}, dimensions={0}, use_global_device_ids=true | all-gather | bytes 270336 | tf_op jit(solution)/shard_map/all_gather | solution.py:13
  260.0 71.4 %all-gather.6.cloned.1.call-done = f32[32,2048,128]{2,1,0:T(8,128)} async-done(((f32[1,2048,128]{2,1,0:T(8,128)}), f32[32,2048,128]{2,1,0:T(8,128)}) %all-gather.6.cloned.1.call-update) | async-done | bytes 33554448 | tf_op jit(solution)/shard_map/all_gather | solution.py:13
  332.7 67.0 %while.34 = (s32[]{:T(128)}, f32[2048]{0:T(1024)S(1)}, f32[2048]{0:T(1024)S(1)}, f32[2048,128]{1,0:T(8,128)S(1)}, f32[32,2048]{1,0:T(8,128)S(1)}, /*index=5*/f32...) while((s32[]{:T(128)}, f32[2048]{0:T(1024)S(1)}, f32[2048]{0:T(1024)S(1)}, ...), condition=%wide.region_6.7_spmd, body=%wide.region_5.6_spmd.sunk | while | flops 798725 | bytes 3260559 | solution.py:18
  332.8 2.1 fusion.35
  334.9 2.1 fusion.35
  337.1 2.1 fusion.35
  339.2 2.1 fusion.35
  341.4 2.1 fusion.35
  (121 shorter events, 63.5 us)
Async XLA Ops:
  6.5 94.3 %copy-start = (bf16[8192,128]{1,0:T(8,128)(2,1)S(1)}, bf16[8192,128]{1,0:T(8,128)(2,1)}, u32[]{:S(2)}) copy-start(bf16[8192,128]{1,0:T(8,128)(2,1)} %param.10) | copy-start | bytes 6291460
  6.5 85.1 %all-gather.8.cloned.1.call-start = ((), (), s32[]{:S(2)}) async-start(), calls=%async_computation.1 | async-start | bytes 17301504 | tf_op jit(solution)/shard_map/all_gather | solution.py:9
  8.2 323.2 %all-gather.6.cloned.1.call-start = ((), (), s32[]{:S(2)}) async-start(), calls=%async_computation | async-start | bytes 34603008 | tf_op jit(solution)/shard_map/all_gather | solution.py:13
Sparse Core Ops, SparseCore 0:
  9.9 81.7 all-gather.7
  212.6 118.7 all-gather.5
